TPU v7x, 32 devices: a whole 2x2x4 slice. The times are simulated.
32 devices in a mesh: parts: 2 (over y), row: 8 (over z, x), col: 2 (over core).
Axes of the slice: x: 2, y: 2, z: 4, core: 2. Of those that a mesh axis runs over, the one named last changes fastest.
Arguments:
- queries: bfloat16 [16384, 256], P(('parts', 'row', 'col')), parts along dimension 0, may hold values from -6 to 6
- counts: int32 [32], P(('parts', 'row', 'col')), parts along dimension 0, may hold values from 1 to 512, as said below
- memory: bfloat16 [512, 256], P(('parts', 'row', 'col')), parts along dimension 0, may hold values from -6 to 6
- mem_mask: int32 [512], P(('parts', 'row', 'col')), parts along dimension 0, may hold values from 0 to 1, as said below
- cross_wq: bfloat16 [256, 256], replicated, may hold values from -0.375 to 0.375
- cross_wkv: bfloat16 [256, 512], replicated, may hold values from -0.375 to 0.375
- cross_wo: bfloat16 [256, 256], replicated, may hold values from -0.375 to 0.375
- self_wqkv: bfloat16 [256, 768], replicated, may hold values from -0.375 to 0.375
- self_wo: bfloat16 [256, 256], replicated, may hold values from -0.375 to 0.375
- ffn_up: bfloat16 [256, 2048], replicated, may hold values from -0.375 to 0.375
- ffn_down: bfloat16 [2048, 256], replicated, may hold values from -0.125 to 0.125
- box_w1: bfloat16 [256, 256], replicated, may hold values from -0.375 to 0.375
- box_w2: bfloat16 [256, 256], replicated, may hold values from -0.375 to 0.375
- box_w3: bfloat16 [256, 4], replicated, may hold values from -0.375 to 0.375
- cross_temp: float32 [8], replicated, may hold values from 1 to 100
- self_temp: float32 [8], replicated, may hold values from 1 to 100
Outputs:
- features: float32 [16384, 256], P(('parts', 'row', 'col')), parts along dimension 0
- boxes: float32 [4, 16384], P(None, ('parts', 'row', 'col')), parts along dimension 1
There are 2 independent parts, one for each index of `parts`. A program takes and returns all parts, laid end to end along the dimension named above; an argument that names none is the same for every part. Nothing has to cross between parts.
Inputs may be any that keep to these rules, and one draw needn't show every extreme that they name: The first counts[t] slots of tile t are live; some tile is full. `mem_mask`: the first memory token of every tile is live.
All inputs are finite; a program needn't handle non-finite values.
Results may differ from a plain program's by a relative error of at most 0.038.
The roundings to bfloat16 on the way count: a program that leaves them out, or rounds other values in their place, can miss the bound.
Values may be sent and summed in bfloat16 or wider, within the bound.
No kernel may reach another device: no remote copies, remote signals or barrier semaphores. Data moves between devices by JAX's collectives and lax.ppermute only.
A program may use at most 64 MiB of HBM per device.

v0:
```python
import functools
import math

import jax
import jax.numpy as jnp
from jax import lax
from jax.experimental import pallas as pl
from jax.experimental.pallas import tpu as pltpu
from jax.sharding import PartitionSpec as P

EPS = 1e-06
DEAD = 64.0
DEAD_V = 4096.0
LOG2E = math.log2(math.e)
LIMIT = 100.0
VMEM = pl.BlockSpec(memory_space=pltpu.VMEM)
SMEM = pl.BlockSpec(memory_space=pltpu.SMEM)
HBM = pl.BlockSpec(memory_space=pltpu.HBM)


def rms_round(x):
    return (x * lax.rsqrt(jnp.mean(x * x, axis=-1, keepdims=True) + EPS)).astype(jnp.bfloat16)


def dot(a, b):
    return jnp.dot(a, b, preferred_element_type=jnp.float32)


def dot_t(a, b):
    return lax.dot_general(a, b, (((1,), (1,)), ((), ())), preferred_element_type=jnp.float32)


def head_of_lane(rows, width, heads):
    return lax.broadcasted_iota(jnp.int32, (rows, width), 1) // (width // heads)


def only(x, head, lane_head):
    return jnp.where(lane_head == head, x, jnp.zeros_like(x))


def flagged(values, flags, head, heads, lane_head):
    other = (head + heads // 2) % heads
    rest = jnp.where(lane_head == other, flags, jnp.zeros_like(values))
    return jnp.where(lane_head == head, values, rest)


def weigh(scores, top, scale):
    return jnp.exp2((scores - top) * scale).astype(jnp.bfloat16)


def normed(low, high):
    half = low.shape[1] // 2
    return jnp.concatenate(
        [low[:, :half] / low[:, half:], high[:, half:] / high[:, :half]], axis=1
    ).astype(jnp.bfloat16)


def mark_kernel(memory, mask, out, held, flags, sems):
    copies = [
        pltpu.make_async_copy(memory, held, sems.at[0]),
        pltpu.make_async_copy(mask, flags, sems.at[1]),
    ]
    for copy in copies:
        copy.start()
    for copy in copies:
        copy.wait()
    row = lax.broadcasted_iota(jnp.int32, held.shape, 0)
    tokens = held[...].astype(jnp.float32)
    for j in range(held.shape[0]):
        tokens = jnp.where((row == j) & (flags[j] <= 0), DEAD, tokens)
    tokens = tokens.astype(jnp.bfloat16)
    for copy in range(out.shape[0]):
        out[copy] = tokens


def load_kernel(
    counts,
    queries,
    wq,
    cross_temp,
    self_temp,
    wkv,
    wo,
    wqkv,
    x_ref,
    qc_ref,
    scale_ref,
    count_ref,
    packed,
    wvt_ref,
    wqt_ref,
    wq_held,
    cross_held,
    self_held,
    sems,
):
    width = x_ref.shape[1]
    pairs = [(queries, x_ref), (wq, wq_held), (cross_temp, cross_held), (self_temp, self_held)]
    begin = 0
    for source in (wkv, wo, wqkv):
        end = begin + source.shape[1]
        pairs.append((source, packed.at[:, begin:end]))
        begin = end
    copies = [pltpu.make_async_copy(a, b, sems.at[i]) for i, (a, b) in enumerate(pairs)]
    for copy in copies:
        copy.start()
    for copy in copies[:4]:
        copy.wait()
    heads = cross_temp.shape[0]
    factor = LOG2E / math.sqrt(width // heads)
    lanes = scale_ref.shape[1]
    for side, temp in enumerate((cross_held, self_held)):
        for head in range(heads):
            at = pl.ds(side * heads + head, 1)
            scale_ref[at, :] = jnp.full((1, lanes), temp[head] * factor, jnp.float32)
    count_ref[...] = jnp.full(count_ref.shape, counts[0], jnp.int32)
    x = x_ref[...].astype(jnp.float32)
    qc_ref[...] = dot(rms_round(x), wq_held[...]).astype(jnp.bfloat16)
    for copy in copies[4:]:
        copy.wait()
    wvt_ref[...] = jnp.transpose(packed[:, -width:])
    wqt_ref[...] = jnp.transpose(packed[:, -3 * width : -2 * width])


def cross_kernel(n, block, tile, heads, scales, counts, queries, qc, *refs):
    pieces = refs[:n]
    packed, wvt, x1_ref, hn_ref, kv_ref, kbd, vbd = refs[n:]
    rows, width = queries.shape
    wkv = packed[:, : 2 * width]
    wo = packed[:, 2 * width : 3 * width]
    wk = packed[:, 4 * width : 5 * width]
    tokens, flags = [], []
    for piece in pieces:
        held = piece[...].astype(jnp.float32)
        dead = held >= DEAD
        for begin in range(0, held.shape[0], tile):
            part = held[begin : begin + tile]
            gone = dead[begin : begin + tile]
            tokens.append(jnp.where(gone, part[:1], part).astype(jnp.bfloat16))
            flags.append(jnp.where(gone, 0.0, 1.0).astype(jnp.bfloat16))
    tokens = jnp.concatenate(tokens, axis=0)
    flags = jnp.concatenate(flags, axis=0)
    count = tokens.shape[0]
    kvm = dot(tokens, wkv).astype(jnp.bfloat16)
    keys = kvm[:, :width]
    values = kvm[:, width:] * flags
    lane_head = head_of_lane(count, width, heads)
    for head in range(heads):
        at = pl.ds(head * count, count)
        kbd[at, :] = only(keys, head, lane_head)
        vbd[at, :] = flagged(values, flags, head, heads, lane_head)
    middle = heads // 2 * count
    for begin in range(0, rows, block):
        at = pl.ds(begin, block)
        x = queries[at, :].astype(jnp.float32)
        scores = dot_t(qc[at, :], kbd[...])
        weights = []
        for head in range(heads):
            s = scores[:, head * count : (head + 1) * count]
            top = jnp.max(s, axis=-1, keepdims=True)
            weights.append(weigh(s, top, scales[head : head + 1, :1]))
        low = dot(jnp.concatenate(weights[: heads // 2], axis=1), vbd[:middle, :])
        high = dot(jnp.concatenate(weights[heads // 2 :], axis=1), vbd[middle:, :])
        x1 = x + dot(normed(low, high), wo)
        x1_ref[at, :] = x1
        hn1 = rms_round(x1)
        hn_ref[at, :] = hn1
        key = dot(hn1, wk).astype(jnp.bfloat16)
        slot = lax.broadcasted_iota(jnp.int32, (block, width), 0) + begin
        if begin == 0:
            first = key[:1]
        kv_ref[at, :] = jnp.where(slot < counts[:1, :1], key, first)
        value = dot_t(wvt[...], hn1).astype(jnp.bfloat16)
        slot = lax.broadcasted_iota(jnp.int32, (width, block), 1) + begin
        value = jnp.where(slot < counts[:1, :1], value, jnp.bfloat16(DEAD_V))
        for part in range(0, block, width):
            place = begin + part
            size = min(block, width)
            target = pl.ds(rows + place // width * width, width)
            lanes = pl.ds(place % width, size)
            kv_ref[target, lanes] = value[:, part : part + size]


def transposed_values(kv, vt, heads):
    rows, width = vt.shape[1], kv.shape[1]
    hsize, part = width // heads, vt.shape[0] // heads
    for begin in range(0, rows, width):
        lanes = pl.ds(begin, width)
        values = kv[rows + begin : rows + begin + width, :]
        live = values < jnp.bfloat16(DEAD_V)
        flags = jnp.where(live[: part - hsize], jnp.bfloat16(1), jnp.bfloat16(0))
        values = jnp.where(live, values, jnp.bfloat16(0))
        for head in range(heads):
            at = head * part
            vt[at : at + hsize, lanes] = values[head * hsize : (head + 1) * hsize]
            vt[at + hsize : at + part, lanes] = flags


def head_rows(width, heads, lanes):
    row = lax.broadcasted_iota(jnp.int32, (width, lanes), 0) // (width // heads)
    lane = lax.broadcasted_iota(jnp.int32, (width, lanes), 1)
    return jnp.where(row == lane, 1.0, 0.0).astype(jnp.bfloat16)


def key_sizes(keys, heads, lanes):
    wide = keys.astype(jnp.float32)
    norms = dot((wide * wide).astype(jnp.bfloat16), head_rows(keys.shape[1], heads, lanes))
    return jnp.max(norms, axis=0, keepdims=True)


def query_sizes(q, scales, heads):
    hsize = q.shape[0] // heads
    lane = lax.broadcasted_iota(jnp.int32, (1, scales.shape[1]), 1)
    sizes = jnp.zeros((1, scales.shape[1]), jnp.float32)
    for head in range(heads):
        part = q[head * hsize : (head + 1) * hsize].astype(jnp.float32)
        norm = jnp.max(jnp.sum(part * part, axis=0, keepdims=True), axis=1, keepdims=True)
        scale = scales[heads + head : heads + head + 1, :]
        sizes = jnp.where(lane == head, norm * scale * scale, sizes)
    return sizes


def half_attention(scales, qt, kv, vt, heads, s_held, p_held, sizes, use):
    rows, width = vt.shape[1], kv.shape[1]
    part = vt.shape[0] // heads
    depth = qt.shape[0] // heads
    per = heads * depth // width
    block = s_held.shape[2]
    units = [(head, begin) for head in range(heads) for begin in range(0, rows, block)]
    bounds = sizes * key_sizes(kv[:rows, :], heads, sizes.shape[1])
    small = jnp.max(bounds) <= LIMIT * LIMIT

    def score(unit):
        head, begin = units[unit]
        lanes = head // per * depth
        q = qt[head * depth : (head + 1) * depth, begin : begin + block]
        return dot(kv[:rows, lanes : lanes + depth], q)

    def scale_of(unit):
        head = units[unit][0]
        return scales[heads + head : heads + head + 1, :1]

    def mix(unit, top):
        head, begin = units[unit]
        total = dot(vt[head * part : (head + 1) * part, :], p_held[unit % 2])
        use(head, pl.ds(begin, block), top, total)

    @pl.when(small)
    def unshifted():
        zero = jnp.zeros((1, block), jnp.float32)
        for step in range(len(units) + 1):
            if step < len(units):
                p_held[step % 2] = jnp.exp2(score(step) * scale_of(step)).astype(jnp.bfloat16)
            if 0 <= step - 1:
                mix(step - 1, zero)

    @pl.when(jnp.logical_not(small))
    def shifted():
        tops = {}
        for step in range(len(units) + 2):
            if step < len(units):
                s = score(step)
                s_held[step % 2] = s
                tops[step] = jnp.max(s, axis=0, keepdims=True)
            last = step - 1
            if 0 <= last < len(units):
                p_held[last % 2] = weigh(s_held[last % 2], tops[last], scale_of(last))
            if 0 <= step - 2:
                mix(step - 2, tops[step - 2])


def own_kernel(
    heads, scales, hn, kv, wqt, qt, top_ref, sum_ref, size_ref, vt, s_held, p_held
):
    width = hn.shape[1]
    hsize = width // heads
    depth = qt.shape[0] // heads
    part = vt.shape[0] // heads
    q = dot_t(wqt[...], hn[...]).astype(jnp.bfloat16)
    sizes = query_sizes(q, scales, heads)
    size_ref[...] = jnp.broadcast_to(sizes, size_ref.shape)
    qt[...] = jnp.zeros_like(qt)
    for head in range(heads):
        begin = head * hsize
        at = head * depth + begin % depth
        qt[at : at + hsize, :] = q[begin : begin + hsize]
    transposed_values(kv, vt, heads)

    def use(head, at, top, total):
        top_ref[head : head + 1, at] = top
        sum_ref[head * part : (head + 1) * part, at] = total

    half_attention(scales, qt, kv, vt, heads, s_held, p_held, sizes, use)


def rest_kernel(
    heads,
    scales,
    counts,
    x1_ref,
    kv,
    qt,
    top_ref,
    sum_ref,
    size_ref,
    wo,
    up,
    down,
    w1,
    w2,
    w3,
    features,
    boxes,
    vt,
    s_held,
    p_held,
    ctx,
    out,
    upper,
    wo_held,
    up_held,
    down_held,
    w1_held,
    w2_held,
    w3_held,
    sems,
):
    rows, width = x1_ref.shape
    hsize = width // heads
    part = vt.shape[0] // heads
    held = (wo_held, up_held, down_held, w1_held, w2_held, w3_held)
    pairs = zip((wo, up, down, w1, w2, w3), held)
    copies = [pltpu.make_async_copy(a, b, sems.at[i]) for i, (a, b) in enumerate(pairs)]
    for copy in copies:
        copy.start()
    transposed_values(kv, vt, heads)

    def use(head, at, top, total):
        scale = scales[heads + head : heads + head + 1, :1]
        first = top_ref[head : head + 1, at]
        most = jnp.maximum(first, top)
        total = total * jnp.exp2((top - most) * scale)
        total += sum_ref[head * part : (head + 1) * part, at] * jnp.exp2((first - most) * scale)
        mixed = total[:hsize] / total[hsize : hsize + 1]
        ctx[head * hsize : (head + 1) * hsize, at] = mixed.astype(jnp.bfloat16)

    half_attention(scales, qt, kv, vt, heads, s_held, p_held, size_ref[:1, :], use)
    for copy in copies:
        copy.wait()
    block = upper.shape[1]
    starts = list(range(0, rows, block))
    ff = up_held.shape[1]
    chunk = ff // 4
    x2, x3, leaves = {}, {}, []

    def project(i):
        at = pl.ds(starts[i], block)
        mixed = lax.dot_general(
            ctx[:, at], wo_held[...], (((0,), (0,)), ((), ())), preferred_element_type=jnp.float32
        )
        x2[i] = x1_ref[at, :] + mixed

    def widen(i):
        hn2 = rms_round(x2[i])
        for begin in range(0, ff, chunk):
            cut = pl.ds(begin, chunk)
            upper[i % 2, :, cut] = jnp.maximum(dot(hn2, up_held[:, cut]), 0.0).astype(jnp.bfloat16)

    def narrow(i):
        at = pl.ds(starts[i], block)
        x3[i] = x2[i] + dot(upper[i % 2], down_held[...])
        slot = lax.broadcasted_iota(jnp.int32, (block, width), 0) + starts[i]
        out[at, :] = jnp.where(slot < counts[:1, :1], x3[i], 0.0)
        leaves.append(
            pltpu.make_async_copy(out.at[at, :], features.at[at, :], sems.at[len(copies) + i])
        )
        leaves[-1].start()

    def box(i):
        b1 = jnp.maximum(dot(rms_round(x3[i]), w1_held[...]), 0.0).astype(jnp.bfloat16)
        b2 = jnp.maximum(dot(b1, w2_held[...]), 0.0).astype(jnp.bfloat16)
        raw = dot_t(w3_held[...], b2)
        slot = lax.broadcasted_iota(jnp.int32, raw.shape, 1) + starts[i]
        boxes[:, pl.ds(starts[i], block)] = jnp.where(
            slot < counts[:1, :1], 1.0 / (1.0 + jnp.exp(-raw)), 0.0
        )

    for step in range(len(starts) + 3):
        for stage, work in enumerate((project, widen, narrow, box)):
            if 0 <= step - stage < len(starts):
                work(step - stage)
    for leave in leaves:
        leave.wait()


def in_hbm(x):
    return pltpu.with_memory_space_constraint(x, pltpu.HBM)


def swap(x, axis):
    size = lax.axis_size(axis)
    return lax.ppermute(x, axis, [(i, i ^ 1) for i in range(size)])


def local(
    queries,
    counts,
    memory,
    mem_mask,
    cross_wq,
    cross_wkv,
    cross_wo,
    self_wqkv,
    self_wo,
    ffn_up,
    ffn_down,
    box_w1,
    box_w2,
    box_w3,
    cross_temp,
    self_temp,
):
    rows, width = queries.shape
    heads = cross_temp.shape[0]
    tile = memory.shape[0]
    params = pltpu.CompilerParams(vmem_limit_bytes=32 * 2**20)
    marked = pl.pallas_call(
        mark_kernel,
        out_shape=pltpu.VMEM((lax.axis_size("row"), tile, width), memory.dtype),
        in_specs=[HBM, HBM],
        out_specs=VMEM,
        scratch_shapes=[
            pltpu.VMEM(memory.shape, memory.dtype),
            pltpu.SMEM(mem_mask.shape, mem_mask.dtype),
            pltpu.SemaphoreType.DMA((2,)),
        ],
        name="mark",
    )(in_hbm(memory), in_hbm(mem_mask))
    gathered = lax.all_to_all(marked, "row", 0, 0, tiled=True)
    pieces = [gathered.reshape(-1, width)]
    tokens = pltpu.VMEM((rows, width), jnp.bfloat16)
    packed_width = cross_wkv.shape[1] + cross_wo.shape[1] + self_wqkv.shape[1]
    sources = (queries, cross_wq, cross_temp, self_temp, cross_wkv, cross_wo, self_wqkv)
    x, qc, scales, live, packed, wvt, wqt = pl.pallas_call(
        load_kernel,
        out_shape=[
            tokens,
            tokens,
            pltpu.VMEM((2 * heads, 128), jnp.float32),
            pltpu.VMEM((8, 128), jnp.int32),
            pltpu.VMEM((width, packed_width), jnp.bfloat16),
            pltpu.VMEM((width, width), jnp.bfloat16),
            pltpu.VMEM((width, width), jnp.bfloat16),
        ],
        in_specs=[SMEM] + [HBM] * len(sources),
        out_specs=[VMEM] * 7,
        scratch_shapes=[
            pltpu.VMEM(cross_wq.shape, cross_wq.dtype),
            pltpu.SMEM(cross_temp.shape, cross_temp.dtype),
            pltpu.SMEM(self_temp.shape, self_temp.dtype),
            pltpu.SemaphoreType.DMA((len(sources),)),
        ],
        compiler_params=params,
        cost_estimate=pl.CostEstimate(
            flops=2 * rows * width * width, bytes_accessed=4 * 2**20, transcendentals=0
        ),
        name="load",
    )(counts, *map(in_hbm, sources))
    count = sum(piece.shape[0] for piece in pieces)
    block = rows if count <= 128 else min(rows, 128)
    kv_shape = pltpu.VMEM((2 * rows, width), jnp.bfloat16)
    x1, hn, kv = pl.pallas_call(
        functools.partial(cross_kernel, len(pieces), block, tile, heads),
        out_shape=(pltpu.VMEM((rows, width), jnp.float32), tokens, kv_shape),
        in_specs=[VMEM] * (6 + len(pieces)),
        out_specs=(VMEM, VMEM, VMEM),
        scratch_shapes=[
            pltpu.VMEM((heads * count, width), jnp.bfloat16),
            pltpu.VMEM((heads * count, width), jnp.bfloat16),
        ],
        compiler_params=params,
        name="cross",
    )(scales, live, x, qc, *pieces, packed, wvt)
    other = swap(kv, "col")
    part = width // heads + 16
    depth = min(128, width)
    block = min(256, rows)
    held = [
        pltpu.VMEM((heads * part, rows), jnp.bfloat16),
        pltpu.VMEM((2, rows, block), jnp.float32),
        pltpu.VMEM((2, rows, block), jnp.bfloat16),
    ]
    qt, tops, sums, sizes = pl.pallas_call(
        functools.partial(own_kernel, heads),
        out_shape=(
            pltpu.VMEM((heads * depth, rows), jnp.bfloat16),
            pltpu.VMEM((heads, rows), jnp.float32),
            pltpu.VMEM((heads * part, rows), jnp.float32),
            pltpu.VMEM((8, 128), jnp.float32),
        ),
        in_specs=[VMEM] * 4,
        out_specs=(VMEM, VMEM, VMEM, VMEM),
        scratch_shapes=held,
        compiler_params=params,
        cost_estimate=pl.CostEstimate(
            flops=8 * heads * rows * rows * width, bytes_accessed=2**20, transcendentals=0
        ),
        name="own",
    )(scales, hn, kv, wqt)
    late = (self_wo, ffn_up, ffn_down, box_w1, box_w2, jnp.transpose(box_w3))
    return pl.pallas_call(
        functools.partial(rest_kernel, heads),
        out_shape=(
            jax.ShapeDtypeStruct((rows, width), jnp.float32),
            jax.ShapeDtypeStruct((box_w3.shape[1], rows), jnp.float32),
        ),
        in_specs=[VMEM] * 8 + [HBM] * len(late),
        out_specs=(HBM, VMEM),
        scratch_shapes=held
        + [
            pltpu.VMEM((width, rows), jnp.bfloat16),
            pltpu.VMEM((rows, width), jnp.float32),
            pltpu.VMEM((2, block, ffn_up.shape[1]), jnp.bfloat16),
        ]
        + [pltpu.VMEM(w.shape, w.dtype) for w in late]
        + [pltpu.SemaphoreType.DMA((len(late) + rows // block,))],
        compiler_params=params,
        name="rest",
    )(scales, live, x1, other, qt, tops, sums, sizes, *map(in_hbm, late))


def solution(mesh):
    return jax.shard_map(
        local,
        mesh=mesh,
        in_specs=(
            P(("parts", "row", "col"), None),
            P(("parts", "row", "col")),
            P(("parts", "row", "col"), None),
            P(("parts", "row", "col")),
            P(),
            P(),
            P(),
            P(),
            P(),
            P(),
            P(),
            P(),
            P(),
            P(),
            P(),
            P(),
        ),
        out_specs=(P(("parts", "row", "col"), None), P(None, ("parts", "row", "col"))),
        check_vma=False,
    )
```

profile of v0, /device:TPU:1, one launch (start us, length us, event | category | flops | bytes accessed | tf_op | source)
XLA Modules:
  0.0 28.4 jit_solution(6980643222936161445)
XLA Ops:
  0.6 1.5 %mark.1 = bf16[8,16,256]{2,1,0:T(8,128)(2,1)} custom-call(bf16[16,256]{1,0:T(8,128)(2,1)} %memory.1, s32[16]{0:T(128)} %mask.1), custom_call_target="tpu_custom_call" | custom-call | tf_op jit(solution)/shard_map/mark/pallas_call | solution.py:427
  2.1 6.4 %all-to-all-start = ((bf16[8,16,256]{2,1,0:T(8,128)(2,1)}), bf16[8,16,256]{2,1,0:T(8,128)(2,1)S(1)}, u32[]{:S(2)}, u32[]{:S(2)}) async-start(bf16[8,16,256]{2,1,0:T(8,128)(2,1)} %mark.1), calls=%async_computation | async-start | bytes 131072 | tf_op jit(solution)/shard_map/all_to_all | solution.py:439
  9.1 1.5 %load.1 = (bf16[512,256]{1,0:T(8,128)(2,1)S(1)}, bf16[512,256]{1,0:T(8,128)(2,1)S(1)}, f32[16,128]{1,0:T(8,128)S(1)}, s32[8,128]{1,0:T(8,128)S(1)}, bf16[256,153...) custom-call(s32[1]{0:T(128)S(6)} %copy.18.counts, bf16[512,256]{1,0:T(8,128)(2,1)} %queries.1, ...), custom_call_target="tpu_custom_call" | custom-call | flops 67108864 | bytes 4194304 | tf_op jit(solution)/shard_map/load/pallas_call | solution.py:444
  10.6 3.6 %all-to-all-done = bf16[8,16,256]{2,1,0:T(8,128)(2,1)S(1)} async-done(((bf16[8,16,256]{2,1,0:T(8,128)(2,1)}), bf16[8,16,256]{2,1,0:T(8,128)(2,1)S(1)}, u32[]{:S(2)}, u32[]{:S(2)}) %all-to-all-start) | async-done | bytes 65568 | tf_op jit(solution)/shard_map/all_to_all | solution.py:439
  14.2 1.5 %cross.1 = (f32[512,256]{1,0:T(8,128)S(1)}, bf16[512,256]{1,0:T(8,128)(2,1)S(1)}, bf16[1024,256]{1,0:T(8,128)(2,1)S(1)}) custom-call(f32[16,128]{1,0:T(8,128)S(1)} %get-tuple-element.16.scales, s32[8,128]{1,0:T(8,128)S(1)} %get-tuple-element.17.counts, bf16[512,256]{1,0:T(8,128)(2,1)S(1)} %get-tuple-element.18.queries, ...), custom_call_target="tpu_custom_call" | custom-call | tf_op jit(solution)/shard_map/cross/pallas_call | solution.py:472
  15.8 2.2 %collective-permute-start = (bf16[1024,256]{1,0:T(8,128)(2,1)S(1)}, bf16[1024,256]{1,0:T(8,128)(2,1)S(1)}, u32[]{:S(2)}, u32[]{:S(2)}) collective-permute-start(bf16[1024,256]{1,0:T(8,128)(2,1)S(1)} %get-tuple-element.23.kv), channel_id=1, source_target_pairs={{0,1},{1,0},{2,3},{3,2},{4,5},{5,4},{6,7},{7,6},{8,9},{9,8},{10,11... | collective-permute-start | bytes 1572872 | tf_op jit(solution)/shard_map/ppermute | solution.py:402
  17.9 3.5 %own.1 = (bf16[1024,512]{1,0:T(8,128)(2,1)S(1)}, f32[8,512]{1,0:T(8,128)S(1)}, f32[384,512]{1,0:T(8,128)S(1)}, f32[8,128]{1,0:T(8,128)S(1)}) custom-call(f32[16,128]{1,0:T(8,128)S(1)} %get-tuple-element.16.scales, bf16[512,256]{1,0:T(8,128)(2,1)S(1)} %get-tuple-element.24.hn, bf16[1024,256]{1,0:T(8,128)(2,1)S(1)} %get-tuple-element.23.kv, ...), custom_call_target="tpu_custom_call" | custom-call | flops 4294967296 | bytes 1048576 | tf_op jit(solution)/shard_map/own/pallas_call | solution.py:493
  21.5 0.0 collective-permute-done.kv
  21.5 6.7 %rest.1 = (f32[512,256]{1,0:T(8,128)}, f32[4,512]{1,0:T(4,128)}) custom-call(f32[16,128]{1,0:T(8,128)S(1)} %get-tuple-element.16.scales, s32[8,128]{1,0:T(8,128)S(1)} %get-tuple-element.17.counts, f32[512,256]{1,0:T(8,128)S(1)} %get-tuple-element.22.x1_ref, bf16[1024,256]{1,0:T(8,128)(2,1)S(1)} %collective-permute-done.kv, ...), custom_call_target="tpu_custom_call" | custom-call | tf_op jit(solution)/shard_map/rest/pallas_call | solution.py:511
Async XLA Ops:
  2.1 12.1 %all-to-all-start = ((bf16[8,16,256]{2,1,0:T(8,128)(2,1)}), bf16[8,16,256]{2,1,0:T(8,128)(2,1)S(1)}, u32[]{:S(2)}, u32[]{:S(2)}) async-start(bf16[8,16,256]{2,1,0:T(8,128)(2,1)} %mark.1), calls=%async_computation | async-start | bytes 131072 | tf_op jit(solution)/shard_map/all_to_all | solution.py:439
  15.8 5.7 %collective-permute-start = (bf16[1024,256]{1,0:T(8,128)(2,1)S(1)}, bf16[1024,256]{1,0:T(8,128)(2,1)S(1)}, u32[]{:S(2)}, u32[]{:S(2)}) collective-permute-start(bf16[1024,256]{1,0:T(8,128)(2,1)S(1)} %get-tuple-element.23.kv), channel_id=1, source_target_pairs={{0,1},{1,0},{2,3},{3,2},{4,5},{5,4},{6,7},{7,6},{8,9},{9,8},{10,11... | collective-permute-start | bytes 1572872 | tf_op jit(solution)/shard_map/ppermute | solution.py:402
where the time goes:
time: 28.7 us; the launch traced here: 28.4 us
  Pallas kernels  14.7 us (51%)
  starting transfers between devices  8.54 us (30%)
  waiting for transfers between devices  3.61 us (13%)
  between operations  1.47 us (5%)
    pallas_call x1, Pallas kernels, local(): pl.pallas_call(functools.partial(rest_kernel, heads), out_shape=(jax.Shap...  6.72 us
    all_to_all x1, starting transfers between devices, local(): gathered = lax.all_to_all(marked, 'row', 0, 0, tiled=True)  6.37 us
    all_to_all x1, waiting for transfers between devices, local(): gathered = lax.all_to_all(marked, 'row', 0, 0, tiled=True)  3.6 us
    pallas_call x1, Pallas kernels, local(): pl.pallas_call(functools.partial(own_kernel, heads), out_shape=(pltpu.VME...  3.54 us
    ppermute x1, starting transfers between devices, swap(): return lax.ppermute(x, axis, [(i, i ^ 1) for i in range(size)])  2.17 us
    pallas_call x1, Pallas kernels, local(): pl.pallas_call(functools.partial(cross_kernel, len(pieces), block, tile,...  1.53 us
    pallas_call x1, Pallas kernels, local(): pl.pallas_call(load_kernel, out_shape=[tokens, tokens, pltpu.VMEM((2 * he...  1.49 us
    pallas_call x1, Pallas kernels, local(): pl.pallas_call(mark_kernel, out_shape=pltpu.VMEM((lax.axis_size('row'), t...  1.46 us
  transfers between devices with their start and end apart: 2, of which 1 were waited for; matrix products, arithmetic and copies ran while one was open for 0% of the time, Pallas kernels for 18%

commit v1 on v0

--- a/solution.py
+++ b/solution.py
@@ -30,29 +30,12 @@
     return lax.dot_general(a, b, (((1,), (1,)), ((), ())), preferred_element_type=jnp.float32)
 
 
-def head_of_lane(rows, width, heads):
-    return lax.broadcasted_iota(jnp.int32, (rows, width), 1) // (width // heads)
-
-
-def only(x, head, lane_head):
-    return jnp.where(lane_head == head, x, jnp.zeros_like(x))
-
-
-def flagged(values, flags, head, heads, lane_head):
-    other = (head + heads // 2) % heads
-    rest = jnp.where(lane_head == other, flags, jnp.zeros_like(values))
-    return jnp.where(lane_head == head, values, rest)
+def dot_l(a, b):
+    return lax.dot_general(a, b, (((0,), (0,)), ((), ())), preferred_element_type=jnp.float32)
 
 
 def weigh(scores, top, scale):
     return jnp.exp2((scores - top) * scale).astype(jnp.bfloat16)
-
-
-def normed(low, high):
-    half = low.shape[1] // 2
-    return jnp.concatenate(
-        [low[:, :half] / low[:, half:], high[:, half:] / high[:, :half]], axis=1
-    ).astype(jnp.bfloat16)
 
 
 def mark_kernel(memory, mask, out, held, flags, sems):
@@ -73,6 +56,16 @@
         out[copy] = tokens
 
 
+def spread(qt, q, heads):
+    depth = qt.shape[0] // heads
+    hsize = q.shape[0] // heads
+    qt[...] = jnp.zeros_like(qt)
+    for head in range(heads):
+        begin = head * hsize
+        at = head * depth + begin % depth
+        qt[at : at + hsize, :] = q[begin : begin + hsize]
+
+
 def load_kernel(
     counts,
     queries,
@@ -83,12 +76,11 @@
     wo,
     wqkv,
     x_ref,
-    qc_ref,
+    qt_ref,
     scale_ref,
     count_ref,
     packed,
-    wvt_ref,
-    wqt_ref,
+    turned,
     wq_held,
     cross_held,
     self_held,
@@ -114,71 +106,58 @@
             at = pl.ds(side * heads + head, 1)
             scale_ref[at, :] = jnp.full((1, lanes), temp[head] * factor, jnp.float32)
     count_ref[...] = jnp.full(count_ref.shape, counts[0], jnp.int32)
-    x = x_ref[...].astype(jnp.float32)
-    qc_ref[...] = dot(rms_round(x), wq_held[...]).astype(jnp.bfloat16)
+    hn0 = rms_round(x_ref[...].astype(jnp.float32))
+    spread(qt_ref, dot_t(jnp.transpose(wq_held[...]), hn0).astype(jnp.bfloat16), heads)
     for copy in copies[4:]:
         copy.wait()
-    wvt_ref[...] = jnp.transpose(packed[:, -width:])
-    wqt_ref[...] = jnp.transpose(packed[:, -3 * width : -2 * width])
-
-
-def cross_kernel(n, block, tile, heads, scales, counts, queries, qc, *refs):
-    pieces = refs[:n]
-    packed, wvt, x1_ref, hn_ref, kv_ref, kbd, vbd = refs[n:]
+    for place, begin in enumerate((width, 3 * width, 5 * width)):
+        turned[place] = jnp.transpose(packed[:, begin : begin + width])
+
+
+def cross_kernel(tile, heads, scales, counts, queries, qt, tokens, packed, turned, *refs):
+    x1_ref, hn_ref, kv_ref, vt, ctx = refs
     rows, width = queries.shape
-    wkv = packed[:, : 2 * width]
-    wo = packed[:, 2 * width : 3 * width]
-    wk = packed[:, 4 * width : 5 * width]
-    tokens, flags = [], []
-    for piece in pieces:
-        held = piece[...].astype(jnp.float32)
-        dead = held >= DEAD
-        for begin in range(0, held.shape[0], tile):
-            part = held[begin : begin + tile]
-            gone = dead[begin : begin + tile]
-            tokens.append(jnp.where(gone, part[:1], part).astype(jnp.bfloat16))
-            flags.append(jnp.where(gone, 0.0, 1.0).astype(jnp.bfloat16))
-    tokens = jnp.concatenate(tokens, axis=0)
-    flags = jnp.concatenate(flags, axis=0)
-    count = tokens.shape[0]
-    kvm = dot(tokens, wkv).astype(jnp.bfloat16)
-    keys = kvm[:, :width]
-    values = kvm[:, width:] * flags
-    lane_head = head_of_lane(count, width, heads)
+    hsize = width // heads
+    part = vt.shape[0] // heads
+    depth = qt.shape[0] // heads
+    per = heads * depth // width
+    held = tokens[...].astype(jnp.float32)
+    dead = held >= DEAD
+    alive = jnp.where(dead, 0.0, held).astype(jnp.bfloat16)
+    flags = jnp.where(dead, 0.0, 1.0).astype(jnp.bfloat16)
+    filled = []
+    for begin in range(0, held.shape[0], tile):
+        piece = held[begin : begin + tile]
+        filled.append(jnp.where(dead[begin : begin + tile], piece[:1], piece))
+    filled = jnp.concatenate(filled, axis=0).astype(jnp.bfloat16)
+    keys = dot(filled, packed[:, :width]).astype(jnp.bfloat16)
+    values = dot_t(turned[0], alive).astype(jnp.bfloat16)
+    first = jnp.where(lax.broadcasted_iota(jnp.int32, (part - hsize, width), 1) == 0, 1.0, 0.0)
+    flags = dot_t(first.astype(jnp.bfloat16), flags).astype(jnp.bfloat16)
     for head in range(heads):
-        at = pl.ds(head * count, count)
-        kbd[at, :] = only(keys, head, lane_head)
-        vbd[at, :] = flagged(values, flags, head, heads, lane_head)
-    middle = heads // 2 * count
-    for begin in range(0, rows, block):
-        at = pl.ds(begin, block)
-        x = queries[at, :].astype(jnp.float32)
-        scores = dot_t(qc[at, :], kbd[...])
-        weights = []
-        for head in range(heads):
-            s = scores[:, head * count : (head + 1) * count]
-            top = jnp.max(s, axis=-1, keepdims=True)
-            weights.append(weigh(s, top, scales[head : head + 1, :1]))
-        low = dot(jnp.concatenate(weights[: heads // 2], axis=1), vbd[:middle, :])
-        high = dot(jnp.concatenate(weights[heads // 2 :], axis=1), vbd[middle:, :])
-        x1 = x + dot(normed(low, high), wo)
-        x1_ref[at, :] = x1
-        hn1 = rms_round(x1)
-        hn_ref[at, :] = hn1
-        key = dot(hn1, wk).astype(jnp.bfloat16)
-        slot = lax.broadcasted_iota(jnp.int32, (block, width), 0) + begin
-        if begin == 0:
-            first = key[:1]
-        kv_ref[at, :] = jnp.where(slot < counts[:1, :1], key, first)
-        value = dot_t(wvt[...], hn1).astype(jnp.bfloat16)
-        slot = lax.broadcasted_iota(jnp.int32, (width, block), 1) + begin
-        value = jnp.where(slot < counts[:1, :1], value, jnp.bfloat16(DEAD_V))
-        for part in range(0, block, width):
-            place = begin + part
-            size = min(block, width)
-            target = pl.ds(rows + place // width * width, width)
-            lanes = pl.ds(place % width, size)
-            kv_ref[target, lanes] = value[:, part : part + size]
+        at = head * part
+        vt[at : at + hsize, :] = values[head * hsize : (head + 1) * hsize]
+        vt[at + hsize : at + part, :] = flags
+    for head in range(heads):
+        lanes = head // per * depth
+        s = dot(keys[:, lanes : lanes + depth], qt[head * depth : (head + 1) * depth, :])
+        top = jnp.max(s, axis=0, keepdims=True)
+        weights = weigh(s, top, scales[head : head + 1, :1])
+        total = dot(vt[head * part : (head + 1) * part, :], weights)
+        mixed = total[:hsize] * (1.0 / total[hsize : hsize + 1])
+        ctx[head * hsize : (head + 1) * hsize, :] = mixed.astype(jnp.bfloat16)
+    x1 = queries[...].astype(jnp.float32) + dot_l(ctx[...], packed[:, 2 * width : 3 * width])
+    x1_ref[...] = x1
+    hn1 = rms_round(x1)
+    hn_ref[...] = hn1
+    key = dot(hn1, packed[:, 4 * width : 5 * width]).astype(jnp.bfloat16)
+    slot = lax.broadcasted_iota(jnp.int32, (rows, width), 0)
+    kv_ref[:rows, :] = jnp.where(slot < counts[:1, :1], key, key[:1])
+    value = dot_t(turned[2], hn1).astype(jnp.bfloat16)
+    slot = lax.broadcasted_iota(jnp.int32, (width, rows), 1)
+    value = jnp.where(slot < counts[:1, :1], value, jnp.bfloat16(DEAD_V))
+    for begin in range(0, rows, width):
+        kv_ref[rows + begin : rows + begin + width, :] = value[:, begin : begin + width]
 
 
 def transposed_values(kv, vt, heads):
@@ -196,28 +175,14 @@
             vt[at + hsize : at + part, lanes] = flags
 
 
-def head_rows(width, heads, lanes):
-    row = lax.broadcasted_iota(jnp.int32, (width, lanes), 0) // (width // heads)
-    lane = lax.broadcasted_iota(jnp.int32, (width, lanes), 1)
-    return jnp.where(row == lane, 1.0, 0.0).astype(jnp.bfloat16)
-
-
-def key_sizes(keys, heads, lanes):
-    wide = keys.astype(jnp.float32)
-    norms = dot((wide * wide).astype(jnp.bfloat16), head_rows(keys.shape[1], heads, lanes))
-    return jnp.max(norms, axis=0, keepdims=True)
-
-
-def query_sizes(q, scales, heads):
-    hsize = q.shape[0] // heads
-    lane = lax.broadcasted_iota(jnp.int32, (1, scales.shape[1]), 1)
-    sizes = jnp.zeros((1, scales.shape[1]), jnp.float32)
-    for head in range(heads):
-        part = q[head * hsize : (head + 1) * hsize].astype(jnp.float32)
-        norm = jnp.max(jnp.sum(part * part, axis=0, keepdims=True), axis=1, keepdims=True)
-        scale = scales[heads + head : heads + head + 1, :]
-        sizes = jnp.where(lane == head, norm * scale * scale, sizes)
-    return sizes
+def largest(q, heads, q_axis):
+    width = q.shape[1 - q_axis]
+    head = lax.broadcasted_iota(jnp.int32, (16, width), 0)
+    lane = lax.broadcasted_iota(jnp.int32, (16, width), 1) // (width // heads)
+    mine = jnp.where(head == lane, 1.0, 0.0).astype(jnp.bfloat16)
+    wide = q.astype(jnp.float32)
+    square = (wide * wide).astype(jnp.bfloat16)
+    return jnp.max((dot if q_axis else dot_t)(mine, square), axis=1, keepdims=True)
 
 
 def half_attention(scales, qt, kv, vt, heads, s_held, p_held, sizes, use):
@@ -227,8 +192,7 @@
     per = heads * depth // width
     block = s_held.shape[2]
     units = [(head, begin) for head in range(heads) for begin in range(0, rows, block)]
-    bounds = sizes * key_sizes(kv[:rows, :], heads, sizes.shape[1])
-    small = jnp.max(bounds) <= LIMIT * LIMIT
+    small = jnp.max(sizes * largest(kv[:rows, :], heads, 0)[:heads]) <= LIMIT * LIMIT
 
     def score(unit):
         head, begin = units[unit]
@@ -270,20 +234,14 @@
 
 
 def own_kernel(
-    heads, scales, hn, kv, wqt, qt, top_ref, sum_ref, size_ref, vt, s_held, p_held
+    heads, scales, hn, kv, turned, qt, top_ref, sum_ref, size_ref, vt, s_held, p_held
 ):
-    width = hn.shape[1]
-    hsize = width // heads
-    depth = qt.shape[0] // heads
     part = vt.shape[0] // heads
-    q = dot_t(wqt[...], hn[...]).astype(jnp.bfloat16)
-    sizes = query_sizes(q, scales, heads)
-    size_ref[...] = jnp.broadcast_to(sizes, size_ref.shape)
-    qt[...] = jnp.zeros_like(qt)
-    for head in range(heads):
-        begin = head * hsize
-        at = head * depth + begin % depth
-        qt[at : at + hsize, :] = q[begin : begin + hsize]
+    q = dot_t(turned[1], hn[...]).astype(jnp.bfloat16)
+    scale = scales[heads : 2 * heads, :]
+    sizes = largest(q, heads, 1)[:heads] * (scale * scale)
+    size_ref[...] = sizes
+    spread(qt, q, heads)
     transposed_values(kv, vt, heads)
 
     def use(head, at, top, total):
@@ -341,24 +299,22 @@
         most = jnp.maximum(first, top)
         total = total * jnp.exp2((top - most) * scale)
         total += sum_ref[head * part : (head + 1) * part, at] * jnp.exp2((first - most) * scale)
-        mixed = total[:hsize] / total[hsize : hsize + 1]
+        mixed = total[:hsize] * (1.0 / total[hsize : hsize + 1])
         ctx[head * hsize : (head + 1) * hsize, at] = mixed.astype(jnp.bfloat16)
 
-    half_attention(scales, qt, kv, vt, heads, s_held, p_held, size_ref[:1, :], use)
+    half_attention(scales, qt, kv, vt, heads, s_held, p_held, size_ref[...], use)
     for copy in copies:
         copy.wait()
     block = upper.shape[1]
     starts = list(range(0, rows, block))
     ff = up_held.shape[1]
     chunk = ff // 4
-    x2, x3, leaves = {}, {}, []
+    x2, x3 = {}, {}
+    leave = pltpu.make_async_copy(out, features, sems.at[len(copies)])
 
     def project(i):
         at = pl.ds(starts[i], block)
-        mixed = lax.dot_general(
-            ctx[:, at], wo_held[...], (((0,), (0,)), ((), ())), preferred_element_type=jnp.float32
-        )
-        x2[i] = x1_ref[at, :] + mixed
+        x2[i] = x1_ref[at, :] + dot_l(ctx[:, at], wo_held[...])
 
     def widen(i):
         hn2 = rms_round(x2[i])
@@ -371,10 +327,8 @@
         x3[i] = x2[i] + dot(upper[i % 2], down_held[...])
         slot = lax.broadcasted_iota(jnp.int32, (block, width), 0) + starts[i]
         out[at, :] = jnp.where(slot < counts[:1, :1], x3[i], 0.0)
-        leaves.append(
-            pltpu.make_async_copy(out.at[at, :], features.at[at, :], sems.at[len(copies) + i])
-        )
-        leaves[-1].start()
+        if i == len(starts) - 1:
+            leave.start()
 
     def box(i):
         b1 = jnp.maximum(dot(rms_round(x3[i]), w1_held[...]), 0.0).astype(jnp.bfloat16)
@@ -389,8 +343,7 @@
         for stage, work in enumerate((project, widen, narrow, box)):
             if 0 <= step - stage < len(starts):
                 work(step - stage)
-    for leave in leaves:
-        leave.wait()
+    leave.wait()
 
 
 def in_hbm(x):
@@ -437,23 +390,24 @@
         name="mark",
     )(in_hbm(memory), in_hbm(mem_mask))
     gathered = lax.all_to_all(marked, "row", 0, 0, tiled=True)
-    pieces = [gathered.reshape(-1, width)]
+    gathered = gathered.reshape(-1, width)
     tokens = pltpu.VMEM((rows, width), jnp.bfloat16)
     packed_width = cross_wkv.shape[1] + cross_wo.shape[1] + self_wqkv.shape[1]
     sources = (queries, cross_wq, cross_temp, self_temp, cross_wkv, cross_wo, self_wqkv)
-    x, qc, scales, live, packed, wvt, wqt = pl.pallas_call(
+    depth = min(128, width)
+    qt_shape = pltpu.VMEM((heads * depth, rows), jnp.bfloat16)
+    x, qt, scales, live, packed, turned = pl.pallas_call(
         load_kernel,
         out_shape=[
             tokens,
-            tokens,
+            qt_shape,
             pltpu.VMEM((2 * heads, 128), jnp.float32),
             pltpu.VMEM((8, 128), jnp.int32),
             pltpu.VMEM((width, packed_width), jnp.bfloat16),
-            pltpu.VMEM((width, width), jnp.bfloat16),
-            pltpu.VMEM((width, width), jnp.bfloat16),
+            pltpu.VMEM((3, width, width), jnp.bfloat16),
         ],
         in_specs=[SMEM] + [HBM] * len(sources),
-        out_specs=[VMEM] * 7,
+        out_specs=[VMEM] * 6,
         scratch_shapes=[
             pltpu.VMEM(cross_wq.shape, cross_wq.dtype),
             pltpu.SMEM(cross_temp.shape, cross_temp.dtype),
@@ -466,24 +420,24 @@
         ),
         name="load",
     )(counts, *map(in_hbm, sources))
-    count = sum(piece.shape[0] for piece in pieces)
-    block = rows if count <= 128 else min(rows, 128)
-    kv_shape = pltpu.VMEM((2 * rows, width), jnp.bfloat16)
+    part = width // heads + 16
     x1, hn, kv = pl.pallas_call(
-        functools.partial(cross_kernel, len(pieces), block, tile, heads),
-        out_shape=(pltpu.VMEM((rows, width), jnp.float32), tokens, kv_shape),
-        in_specs=[VMEM] * (6 + len(pieces)),
+        functools.partial(cross_kernel, tile, heads),
+        out_shape=(
+            pltpu.VMEM((rows, width), jnp.float32),
+            tokens,
+            pltpu.VMEM((2 * rows, width), jnp.bfloat16),
+        ),
+        in_specs=[VMEM] * 7,
         out_specs=(VMEM, VMEM, VMEM),
         scratch_shapes=[
-            pltpu.VMEM((heads * count, width), jnp.bfloat16),
-            pltpu.VMEM((heads * count, width), jnp.bfloat16),
+            pltpu.VMEM((heads * part, gathered.shape[0]), jnp.bfloat16),
+            pltpu.VMEM((width, rows), jnp.bfloat16),
         ],
         compiler_params=params,
         name="cross",
-    )(scales, live, x, qc, *pieces, packed, wvt)
+    )(scales, live, x, qt, gathered, packed, turned)
     other = swap(kv, "col")
-    part = width // heads + 16
-    depth = min(128, width)
     block = min(256, rows)
     held = [
         pltpu.VMEM((heads * part, rows), jnp.bfloat16),
@@ -493,10 +447,10 @@
     qt, tops, sums, sizes = pl.pallas_call(
         functools.partial(own_kernel, heads),
         out_shape=(
-            pltpu.VMEM((heads * depth, rows), jnp.bfloat16),
+            qt_shape,
             pltpu.VMEM((heads, rows), jnp.float32),
             pltpu.VMEM((heads * part, rows), jnp.float32),
-            pltpu.VMEM((8, 128), jnp.float32),
+            pltpu.VMEM((heads, 128), jnp.float32),
         ),
         in_specs=[VMEM] * 4,
         out_specs=(VMEM, VMEM, VMEM, VMEM),
@@ -506,7 +460,7 @@
             flops=8 * heads * rows * rows * width, bytes_accessed=2**20, transcendentals=0
         ),
         name="own",
-    )(scales, hn, kv, wqt)
+    )(scales, hn, kv, turned)
     late = (self_wo, ffn_up, ffn_down, box_w1, box_w2, jnp.transpose(box_w3))
     return pl.pallas_call(
         functools.partial(rest_kernel, heads),
@@ -523,7 +477,7 @@
             pltpu.VMEM((2, block, ffn_up.shape[1]), jnp.bfloat16),
         ]
         + [pltpu.VMEM(w.shape, w.dtype) for w in late]
-        + [pltpu.SemaphoreType.DMA((len(late) + rows // block,))],
+        + [pltpu.SemaphoreType.DMA((len(late) + 1,))],
         compiler_params=params,
         name="rest",
     )(scales, live, x1, other, qt, tops, sums, sizes, *map(in_hbm, late))

time: 28.7 us -> 29.8 us (1.038)
  Pallas kernels: 14.7 us -> 16 us
    pallas_call x3, Pallas kernels: 6.56 us -> 7.7 us  [the longest x1 3.65 us: local(): pl.pallas_call(functools.partial(own_kernel, heads), out_shape=(qt_shape,...]
where the time goes in v1:
time: 29.8 us; the launch traced here: 29.5 us
  Pallas kernels  16 us (54%)
  starting transfers between devices  8.54 us (29%)
  waiting for transfers between devices  3.51 us (12%)
  between operations  1.47 us (5%)
    pallas_call x1, Pallas kernels, local(): pl.pallas_call(functools.partial(rest_kernel, heads), out_shape=(jax.Shap...  6.82 us
    all_to_all x1, starting transfers between devices, local(): gathered = lax.all_to_all(marked, 'row', 0, 0, tiled=True)  6.37 us
    pallas_call x1, Pallas kernels, local(): pl.pallas_call(functools.partial(own_kernel, heads), out_shape=(qt_shape,...  3.65 us
    all_to_all x1, waiting for transfers between devices, local(): gathered = lax.all_to_all(marked, 'row', 0, 0, tiled=True)  3.51 us
    pallas_call x1, Pallas kernels, local(): pl.pallas_call(functools.partial(cross_kernel, tile, heads), out_shape=(p...  2.46 us
    ppermute x1, starting transfers between devices, swap(): return lax.ppermute(x, axis, [(i, i ^ 1) for i in range(size)])  2.17 us
    pallas_call x1, Pallas kernels, local(): pl.pallas_call(load_kernel, out_shape=[tokens, qt_shape, pltpu.VMEM((2 *...  1.59 us
    pallas_call x1, Pallas kernels, local(): pl.pallas_call(mark_kernel, out_shape=pltpu.VMEM((lax.axis_size('row'), t...  1.46 us
  transfers between devices with their start and end apart: 2, of which 1 were waited for; matrix products, arithmetic and copies ran while one was open for 0% of the time, Pallas kernels for 18%

profile of v1, /device:TPU:1, one launch (start us, length us, event | category | flops | bytes accessed | tf_op | source)
XLA Modules:
  0.0 29.5 jit_solution(2628789034666758459)
XLA Ops:
  0.6 1.5 %mark.1 = bf16[8,16,256]{2,1,0:T(8,128)(2,1)} custom-call(bf16[16,256]{1,0:T(8,128)(2,1)} %memory.1, s32[16]{0:T(128)} %mask.1), custom_call_target="tpu_custom_call" | custom-call | tf_op jit(solution)/shard_map/mark/pallas_call | solution.py:380
  2.1 6.4 %all-to-all-start = ((bf16[8,16,256]{2,1,0:T(8,128)(2,1)}), bf16[8,16,256]{2,1,0:T(8,128)(2,1)S(1)}, u32[]{:S(2)}, u32[]{:S(2)}) async-start(bf16[8,16,256]{2,1,0:T(8,128)(2,1)} %mark.1), calls=%async_computation | async-start | bytes 131072 | tf_op jit(solution)/shard_map/all_to_all | solution.py:392
  9.1 1.6 %load.1 = (bf16[512,256]{1,0:T(8,128)(2,1)S(1)}, bf16[1024,512]{1,0:T(8,128)(2,1)S(1)}, f32[16,128]{1,0:T(8,128)S(1)}, s32[8,128]{1,0:T(8,128)S(1)}, bf16[256,15...) custom-call(s32[1]{0:T(128)S(6)} %copy.18.counts, bf16[512,256]{1,0:T(8,128)(2,1)} %queries.1, bf16[256,256]{1,0:T(8,128)(2,1)} %wq.1, ...), custom_call_target="tpu_custom_call" | custom-call | flops 67108864 | bytes 4194304 | tf_op jit(solution)/shard_map/load/pallas_call | solution.py:399
  10.7 3.5 %all-to-all-done = bf16[8,16,256]{2,1,0:T(8,128)(2,1)S(1)} async-done(((bf16[8,16,256]{2,1,0:T(8,128)(2,1)}), bf16[8,16,256]{2,1,0:T(8,128)(2,1)S(1)}, u32[]{:S(2)}, u32[]{:S(2)}) %all-to-all-start) | async-done | bytes 65568 | tf_op jit(solution)/shard_map/all_to_all | solution.py:392
  14.2 2.5 %cross.1 = (f32[512,256]{1,0:T(8,128)S(1)}, bf16[512,256]{1,0:T(8,128)(2,1)S(1)}, bf16[1024,256]{1,0:T(8,128)(2,1)S(1)}) custom-call(f32[16,128]{1,0:T(8,128)S(1)} %get-tuple-element.15.scales, s32[8,128]{1,0:T(8,128)S(1)} %get-tuple-element.16.counts, bf16[512,256]{1,0:T(8,128)(2,1)S(1)} %get-tuple-element.17.queries, ...), custom_call_target="tpu_custom_call" | custom-call | tf_op jit(solution)/shard_map/cross/pallas_call | solution.py:424
  16.7 2.2 %collective-permute-start = (bf16[1024,256]{1,0:T(8,128)(2,1)S(1)}, bf16[1024,256]{1,0:T(8,128)(2,1)S(1)}, u32[]{:S(2)}, u32[]{:S(2)}) collective-permute-start(bf16[1024,256]{1,0:T(8,128)(2,1)S(1)} %get-tuple-element.22.kv), channel_id=1, source_target_pairs={{0,1},{1,0},{2,3},{3,2},{4,5},{5,4},{6,7},{7,6},{8,9},{9,8},{10,11... | collective-permute-start | bytes 1572872 | tf_op jit(solution)/shard_map/ppermute | solution.py:355
  18.9 3.7 %own.1 = (bf16[1024,512]{1,0:T(8,128)(2,1)S(1)}, f32[8,512]{1,0:T(8,128)S(1)}, f32[384,512]{1,0:T(8,128)S(1)}, f32[8,128]{1,0:T(8,128)S(1)}) custom-call(f32[16,128]{1,0:T(8,128)S(1)} %get-tuple-element.15.scales, bf16[512,256]{1,0:T(8,128)(2,1)S(1)} %get-tuple-element.23.hn, bf16[1024,256]{1,0:T(8,128)(2,1)S(1)} %get-tuple-element.22.kv, ...), custom_call_target="tpu_custom_call" | custom-call | flops 4294967296 | bytes 1048576 | tf_op jit(solution)/shard_map/own/pallas_call | solution.py:447
  22.5 0.0 collective-permute-done.kv
  22.5 6.8 %rest.1 = (f32[512,256]{1,0:T(8,128)}, f32[4,512]{1,0:T(4,128)}) custom-call(f32[16,128]{1,0:T(8,128)S(1)} %get-tuple-element.15.scales, s32[8,128]{1,0:T(8,128)S(1)} %get-tuple-element.16.counts, f32[512,256]{1,0:T(8,128)S(1)} %get-tuple-element.21.x1_ref, bf16[1024,256]{1,0:T(8,128)(2,1)S(1)} %collective-permute-done.kv, ...), custom_call_target="tpu_custom_call" | custom-call | tf_op jit(solution)/shard_map/rest/pallas_call | solution.py:465
Async XLA Ops:
  2.1 12.1 %all-to-all-start = ((bf16[8,16,256]{2,1,0:T(8,128)(2,1)}), bf16[8,16,256]{2,1,0:T(8,128)(2,1)S(1)}, u32[]{:S(2)}, u32[]{:S(2)}) async-start(bf16[8,16,256]{2,1,0:T(8,128)(2,1)} %mark.1), calls=%async_computation | async-start | bytes 131072 | tf_op jit(solution)/shard_map/all_to_all | solution.py:392
  16.7 5.8 %collective-permute-start = (bf16[1024,256]{1,0:T(8,128)(2,1)S(1)}, bf16[1024,256]{1,0:T(8,128)(2,1)S(1)}, u32[]{:S(2)}, u32[]{:S(2)}) collective-permute-start(bf16[1024,256]{1,0:T(8,128)(2,1)S(1)} %get-tuple-element.22.kv), channel_id=1, source_target_pairs={{0,1},{1,0},{2,3},{3,2},{4,5},{5,4},{6,7},{7,6},{8,9},{9,8},{10,11... | collective-permute-start | bytes 1572872 | tf_op jit(solution)/shard_map/ppermute | solution.py:355

commit v2 on v0

--- a/solution.py
+++ b/solution.py
@@ -11,8 +11,7 @@
 EPS = 1e-06
 DEAD = 64.0
 DEAD_V = 4096.0
-LOG2E = math.log2(math.e)
-LIMIT = 100.0
+LIMIT = 69.0
 VMEM = pl.BlockSpec(memory_space=pltpu.VMEM)
 SMEM = pl.BlockSpec(memory_space=pltpu.SMEM)
 HBM = pl.BlockSpec(memory_space=pltpu.HBM)
@@ -45,7 +44,7 @@
 
 
 def weigh(scores, top, scale):
-    return jnp.exp2((scores - top) * scale).astype(jnp.bfloat16)
+    return jnp.exp((scores - top) * scale).astype(jnp.bfloat16)
 
 
 def normed(low, high):
@@ -107,7 +106,7 @@
     for copy in copies[:4]:
         copy.wait()
     heads = cross_temp.shape[0]
-    factor = LOG2E / math.sqrt(width // heads)
+    factor = 1.0 / math.sqrt(width // heads)
     lanes = scale_ref.shape[1]
     for side, temp in enumerate((cross_held, self_held)):
         for head in range(heads):
@@ -250,7 +249,7 @@
         zero = jnp.zeros((1, block), jnp.float32)
         for step in range(len(units) + 1):
             if step < len(units):
-                p_held[step % 2] = jnp.exp2(score(step) * scale_of(step)).astype(jnp.bfloat16)
+                p_held[step % 2] = jnp.exp(score(step) * scale_of(step)).astype(jnp.bfloat16)
             if 0 <= step - 1:
                 mix(step - 1, zero)
 
@@ -339,8 +338,8 @@
         scale = scales[heads + head : heads + head + 1, :1]
         first = top_ref[head : head + 1, at]
         most = jnp.maximum(first, top)
-        total = total * jnp.exp2((top - most) * scale)
-        total += sum_ref[head * part : (head + 1) * part, at] * jnp.exp2((first - most) * scale)
+        total = total * jnp.exp((top - most) * scale)
+        total += sum_ref[head * part : (head + 1) * part, at] * jnp.exp((first - most) * scale)
         mixed = total[:hsize] / total[hsize : hsize + 1]
         ctx[head * hsize : (head + 1) * hsize, at] = mixed.astype(jnp.bfloat16)
 

time: 28.7 us -> 29.4 us (1.024)
  Pallas kernels: 14.7 us -> 15.5 us
    pallas_call x1, Pallas kernels: 6.72 us -> 7.12 us  [local(): pl.pallas_call(functools.partial(rest_kernel, heads), out_shape=(jax.Shap...]
    pallas_call x1, Pallas kernels: 3.54 us -> 3.88 us  [local(): pl.pallas_call(functools.partial(own_kernel, heads), out_shape=(pltpu.VME...]
where the time goes in v2:
time: 29.4 us; the launch traced here: 29.1 us
  Pallas kernels  15.5 us (53%)
  starting transfers between devices  8.54 us (29%)
  waiting for transfers between devices  3.61 us (12%)
  between operations  1.47 us (5%)
    pallas_call x1, Pallas kernels, local(): pl.pallas_call(functools.partial(rest_kernel, heads), out_shape=(jax.Shap...  7.12 us
    all_to_all x1, starting transfers between devices, local(): gathered = lax.all_to_all(marked, 'row', 0, 0, tiled=True)  6.37 us
    pallas_call x1, Pallas kernels, local(): pl.pallas_call(functools.partial(own_kernel, heads), out_shape=(pltpu.VME...  3.88 us
    all_to_all x1, waiting for transfers between devices, local(): gathered = lax.all_to_all(marked, 'row', 0, 0, tiled=True)  3.6 us
    ppermute x1, starting transfers between devices, swap(): return lax.ppermute(x, axis, [(i, i ^ 1) for i in range(size)])  2.17 us
    pallas_call x1, Pallas kernels, local(): pl.pallas_call(functools.partial(cross_kernel, len(pieces), block, tile,...  1.54 us
    pallas_call x1, Pallas kernels, local(): pl.pallas_call(load_kernel, out_shape=[tokens, tokens, pltpu.VMEM((2 * he...  1.49 us
    pallas_call x1, Pallas kernels, local(): pl.pallas_call(mark_kernel, out_shape=pltpu.VMEM((lax.axis_size('row'), t...  1.46 us
  transfers between devices with their start and end apart: 2, of which 1 were waited for; matrix products, arithmetic and copies ran while one was open for 0% of the time, Pallas kernels for 18%

profile of v2, /device:TPU:1, one launch (start us, length us, event | category | flops | bytes accessed | tf_op | source)
XLA Modules:
  0.0 29.1 jit_solution(3422244943190116490)
XLA Ops:
  0.6 1.5 %mark.1 = bf16[8,16,256]{2,1,0:T(8,128)(2,1)} custom-call(bf16[16,256]{1,0:T(8,128)(2,1)} %memory.1, s32[16]{0:T(128)} %mask.1), custom_call_target="tpu_custom_call" | custom-call | tf_op jit(solution)/shard_map/mark/pallas_call | solution.py:426
  2.1 6.4 %all-to-all-start = ((bf16[8,16,256]{2,1,0:T(8,128)(2,1)}), bf16[8,16,256]{2,1,0:T(8,128)(2,1)S(1)}, u32[]{:S(2)}, u32[]{:S(2)}) async-start(bf16[8,16,256]{2,1,0:T(8,128)(2,1)} %mark.1), calls=%async_computation | async-start | bytes 131072 | tf_op jit(solution)/shard_map/all_to_all | solution.py:438
  9.1 1.5 %load.1 = (bf16[512,256]{1,0:T(8,128)(2,1)S(1)}, bf16[512,256]{1,0:T(8,128)(2,1)S(1)}, f32[16,128]{1,0:T(8,128)S(1)}, s32[8,128]{1,0:T(8,128)S(1)}, bf16[256,153...) custom-call(s32[1]{0:T(128)S(6)} %copy.18.counts, bf16[512,256]{1,0:T(8,128)(2,1)} %queries.1, ...), custom_call_target="tpu_custom_call" | custom-call | flops 67108864 | bytes 4194304 | tf_op jit(solution)/shard_map/load/pallas_call | solution.py:443
  10.6 3.6 %all-to-all-done = bf16[8,16,256]{2,1,0:T(8,128)(2,1)S(1)} async-done(((bf16[8,16,256]{2,1,0:T(8,128)(2,1)}), bf16[8,16,256]{2,1,0:T(8,128)(2,1)S(1)}, u32[]{:S(2)}, u32[]{:S(2)}) %all-to-all-start) | async-done | bytes 65568 | tf_op jit(solution)/shard_map/all_to_all | solution.py:438
  14.2 1.5 %cross.1 = (f32[512,256]{1,0:T(8,128)S(1)}, bf16[512,256]{1,0:T(8,128)(2,1)S(1)}, bf16[1024,256]{1,0:T(8,128)(2,1)S(1)}) custom-call(f32[16,128]{1,0:T(8,128)S(1)} %get-tuple-element.16.scales, s32[8,128]{1,0:T(8,128)S(1)} %get-tuple-element.17.counts, bf16[512,256]{1,0:T(8,128)(2,1)S(1)} %get-tuple-element.18.queries, ...), custom_call_target="tpu_custom_call" | custom-call | tf_op jit(solution)/shard_map/cross/pallas_call | solution.py:471
  15.8 2.2 %collective-permute-start = (bf16[1024,256]{1,0:T(8,128)(2,1)S(1)}, bf16[1024,256]{1,0:T(8,128)(2,1)S(1)}, u32[]{:S(2)}, u32[]{:S(2)}) collective-permute-start(bf16[1024,256]{1,0:T(8,128)(2,1)S(1)} %get-tuple-element.23.kv), channel_id=1, source_target_pairs={{0,1},{1,0},{2,3},{3,2},{4,5},{5,4},{6,7},{7,6},{8,9},{9,8},{10,11... | collective-permute-start | bytes 1572872 | tf_op jit(solution)/shard_map/ppermute | solution.py:401
  17.9 3.9 %own.1 = (bf16[1024,512]{1,0:T(8,128)(2,1)S(1)}, f32[8,512]{1,0:T(8,128)S(1)}, f32[384,512]{1,0:T(8,128)S(1)}, f32[8,128]{1,0:T(8,128)S(1)}) custom-call(f32[16,128]{1,0:T(8,128)S(1)} %get-tuple-element.16.scales, bf16[512,256]{1,0:T(8,128)(2,1)S(1)} %get-tuple-element.24.hn, bf16[1024,256]{1,0:T(8,128)(2,1)S(1)} %get-tuple-element.23.kv, ...), custom_call_target="tpu_custom_call" | custom-call | flops 4294967296 | bytes 1048576 | tf_op jit(solution)/shard_map/own/pallas_call | solution.py:492
  21.8 0.0 collective-permute-done.kv
  21.8 7.1 %rest.1 = (f32[512,256]{1,0:T(8,128)}, f32[4,512]{1,0:T(4,128)}) custom-call(f32[16,128]{1,0:T(8,128)S(1)} %get-tuple-element.16.scales, s32[8,128]{1,0:T(8,128)S(1)} %get-tuple-element.17.counts, f32[512,256]{1,0:T(8,128)S(1)} %get-tuple-element.22.x1_ref, bf16[1024,256]{1,0:T(8,128)(2,1)S(1)} %collective-permute-done.kv, ...), custom_call_target="tpu_custom_call" | custom-call | tf_op jit(solution)/shard_map/rest/pallas_call | solution.py:510
Async XLA Ops:
  2.1 12.1 %all-to-all-start = ((bf16[8,16,256]{2,1,0:T(8,128)(2,1)}), bf16[8,16,256]{2,1,0:T(8,128)(2,1)S(1)}, u32[]{:S(2)}, u32[]{:S(2)}) async-start(bf16[8,16,256]{2,1,0:T(8,128)(2,1)} %mark.1), calls=%async_computation | async-start | bytes 131072 | tf_op jit(solution)/shard_map/all_to_all | solution.py:438
  15.8 6.1 %collective-permute-start = (bf16[1024,256]{1,0:T(8,128)(2,1)S(1)}, bf16[1024,256]{1,0:T(8,128)(2,1)S(1)}, u32[]{:S(2)}, u32[]{:S(2)}) collective-permute-start(bf16[1024,256]{1,0:T(8,128)(2,1)S(1)} %get-tuple-element.23.kv), channel_id=1, source_target_pairs={{0,1},{1,0},{2,3},{3,2},{4,5},{5,4},{6,7},{7,6},{8,9},{9,8},{10,11... | collective-permute-start | bytes 1572872 | tf_op jit(solution)/shard_map/ppermute | solution.py:401
